TPU v7x, 512 devices: a whole 4x4x16 slice. The times are simulated.
512 devices in a mesh: row: 16 (over x, y_lo, core), col: 32 (over z, y_hi).
Axes of the slice: x: 4, y: 4 (y_hi: 2, y_lo: 2; y = y_hi * 2 + y_lo), z: 16, core: 2. Of those that a mesh axis runs over, the one named last changes fastest.
Arguments:
- features: bfloat16 [128, 1024, 256], P('row', 'col'), may hold values from -16 to 16
- expand_weight: bfloat16 [2, 256, 1024], replicated, may hold values from -0.375 to 0.375
- expand_bias: float32 [2, 1024], replicated, may hold values from -3 to 3
- depth_weight: float32 [2, 3, 3, 1024], replicated, may hold values from -2 to 2
- depth_bias: float32 [2, 1024], replicated, may hold values from -3 to 3
- project_weight: bfloat16 [2, 1024, 256], replicated, may hold values from -0.1875 to 0.1875
- project_bias: float32 [2, 256], replicated, may hold values from -3 to 3
- qkv_weight: bfloat16 [2, 256, 768], replicated, may hold values from -0.375 to 0.375
- aggregate_depth: float32 [2, 5, 5, 768], replicated, may hold values from -1.25 to 1.25
- aggregate_group: bfloat16 [2, 24, 32, 32], replicated, may hold values from -1 to 1
- output_weight: bfloat16 [2, 512, 256], replicated, may hold values from -0.25 to 0.25
- output_bias: float32 [2, 256], replicated, may hold values from -3 to 3
- head_weight: bfloat16 [3, 3, 4, 256], replicated, may hold values from -0.125 to 0.125
- head_bias: float32 [4], replicated, may hold values from -3 to 3
Outputs:
- final_map: bfloat16 [128, 1024, 256], P('row', 'col')
- boxes: float32 [4, 128, 1024], P(None, 'row', 'col')
All inputs are finite; a program needn't handle non-finite values.
Results may differ from a plain program's by a relative error of at most 0.009.
Values may be sent and summed in bfloat16 or wider, within the bound.
A program may use at most 64 MiB of HBM per device.

v0:
```python
import jax
import jax.numpy as jnp
from jax import lax
from jax.sharding import PartitionSpec as P

SECTIONS = 2


def with_halo(cells, sides, width):
    for axis, dim in sides:
        count = lax.axis_size(axis)
        ends = count - 1
        head = lax.slice_in_dim(cells, 0, width, axis=dim)
        tail = lax.slice_in_dim(cells, cells.shape[dim] - width, cells.shape[dim], axis=dim)
        cells = jnp.concatenate(
            [
                lax.ppermute(tail, axis, [(i, (i + 1) % count) for i in range(ends)]),
                cells,
                lax.ppermute(head, axis, [((i + 1) % count, i) for i in range(ends)]),
            ],
            axis=dim,
        )
    return cells


def hard_swish(value):
    return value * jnp.minimum(jnp.maximum(value + 3.0, 0.0), 6.0) / 6.0


def depthwise(padded, weight, rows, cols):
    ksize = weight.shape[0]
    total = jnp.zeros((rows, cols, padded.shape[2]), jnp.float32)
    for offset_r in range(ksize):
        for offset_c in range(ksize):
            total = (
                total
                + padded[offset_r : offset_r + rows, offset_c : offset_c + cols, :].astype(
                    jnp.float32
                )
                * weight[offset_r, offset_c]
            )
    return total


def dense(values, weight):
    return lax.dot_general(
        values, weight, (((values.ndim - 1,), (0,)), ((), ())), preferred_element_type=jnp.float32
    )


def heads_of(padded_qkv, agg_depth, agg_group, rows, cols, heads, head_dim):
    center = padded_qkv[2 : 2 + rows, 2 : 2 + cols, :]
    spread = depthwise(padded_qkv, agg_depth, rows, cols).astype(jnp.bfloat16)
    grouped = jnp.einsum(
        "rcgd,gde->rcge",
        spread.reshape(rows, cols, 3 * heads, head_dim),
        agg_group,
        preferred_element_type=jnp.float32,
    ).astype(jnp.bfloat16)
    return jnp.concatenate(
        [
            center.reshape(rows, cols, heads, 3, head_dim),
            grouped.reshape(rows, cols, heads, 3, head_dim),
        ],
        axis=2,
    )


def local(
    features,
    expand_weight,
    expand_bias,
    depth_weight,
    depth_bias,
    project_weight,
    project_bias,
    qkv_weight,
    aggregate_depth,
    aggregate_group,
    output_weight,
    output_bias,
    head_weight,
    head_bias,
):
    rows, cols, width = features.shape
    head_dim = aggregate_group.shape[2]
    heads = width // head_dim
    current = features
    for section in range(SECTIONS):
        hidden = hard_swish(dense(current, expand_weight[section]) + expand_bias[section]).astype(
            jnp.bfloat16
        )
        hidden = with_halo(hidden, (("row", 0), ("col", 1)), 1)
        spread = hard_swish(
            depthwise(hidden, depth_weight[section], rows, cols) + depth_bias[section]
        ).astype(jnp.bfloat16)
        mixed = (current + dense(spread, project_weight[section]) + project_bias[section]).astype(
            jnp.bfloat16
        )
        local_qkv = dense(mixed, qkv_weight[section]).astype(jnp.bfloat16)
        padded_qkv = with_halo(local_qkv, (("row", 0), ("col", 1)), 2)
        both = heads_of(
            padded_qkv,
            aggregate_depth[section],
            aggregate_group[section],
            rows,
            cols,
            heads,
            head_dim,
        )
        queries = jax.nn.relu(both[:, :, :, 0, :]).astype(jnp.float32)
        keys = jax.nn.relu(both[:, :, :, 1, :]).astype(jnp.float32)
        values = both[:, :, :, 2, :].astype(jnp.float32)
        kv_local = jnp.einsum("rchd,rche->hde", keys, values, precision=lax.Precision.HIGHEST)
        key_local = jnp.sum(keys, axis=(0, 1))
        kv_all, key_all = lax.psum((kv_local, key_local), ("row", "col"))
        numer = jnp.einsum("rchd,hde->rche", queries, kv_all, precision=lax.Precision.HIGHEST)
        denom = jnp.einsum("rchd,hd->rch", queries, key_all, precision=lax.Precision.HIGHEST)
        attended = (
            (numer / (denom[..., None] + 1e-06)).astype(jnp.bfloat16).reshape(rows, cols, 2 * width)
        )
        current = (mixed + dense(attended, output_weight[section]) + output_bias[section]).astype(
            jnp.bfloat16
        )
    padded = with_halo(current, (("row", 0), ("col", 1)), 1)
    boxes = jnp.zeros((4, rows, cols), jnp.float32)
    for offset_r in range(3):
        for offset_c in range(3):
            window = padded[offset_r : offset_r + rows, offset_c : offset_c + cols, :]
            boxes = boxes + lax.dot_general(
                head_weight[offset_r, offset_c],
                window,
                (((1,), (2,)), ((), ())),
                preferred_element_type=jnp.float32,
            )
    boxes = boxes + head_bias[:, None, None]
    return (current, boxes)


def solution(mesh):
    return jax.shard_map(
        local,
        mesh=mesh,
        in_specs=(
            P("row", "col", None),
            P(),
            P(),
            P(),
            P(),
            P(),
            P(),
            P(),
            P(),
            P(),
            P(),
            P(),
            P(),
            P(),
        ),
        out_specs=(P("row", "col", None), P(None, "row", "col")),
        check_vma=False,
    )
```

profile of v0, /device:TPU:1, one launch (start us, length us, event | category | flops | bytes accessed | tf_op | source)
XLA Modules:
  0.0 1291.3 jit_solution(16654592046291332820)
XLA Ops:
  7.3 1.4 fusion.129
  8.6 1.5 multiply_convert_fusion.3
  10.1 4.6 collective-permute-start
  14.7 5.5 collective-permute-start.1
  23.1 1.9 collective-permute-start.2
  24.9 1.3 collective-permute-start.3
  27.0 4.2 collective-permute-done.3
  31.6 1.5 fusion.11
  34.1 3.7 collective-permute-start.4
  37.8 1.9 collective-permute-start.5
  40.4 1.6 reshape.49
  42.0 2.0 collective-permute-done.5
  44.0 6.0 collective-permute-start.6
  51.3 1.9 copy_dynamic-update-slice_fusion.3
  53.3 2.9 collective-permute-done.7
  56.7 3.0 add_convert_fusion.1
  61.3 1.3 copy-done
  63.4 1.4 copy-done.1
  66.0 111.1 %psum.29 = f32[16,32]{1,0:T(8,128)S(1)} all-reduce(f32[16,32]{1,0:T(8,128)S(1)} %convert_reduce_fusion.1), channel_id=1, replica_groups=mesh['row'=16,'col'=32] {'row','col'}, use_global_device_ids=true, to_apply=%region_2.3 | all-reduce | flops 512 | bytes 4096 | tf_op jit(solution)/shard_map/psum | solution.py:116
  177.0 5.4 fusion.26
  182.5 450.1 %all-reduce.3.cloned.1.call-done = f32[16,32,32]{1,2,0:T(8,128)} async-done(((f32[16,32,32]{1,2,0:T(8,128)}), f32[16,32,32]{1,2,0:T(8,128)}) %all-reduce.3.cloned.1.call-update) | async-done | bytes 65552 | tf_op jit(solution)/shard_map/psum | solution.py:116
  632.6 6.1 fusion.1
  642.4 4.9 collective-permute-start.8
  647.3 1.9 collective-permute-start.9
  649.3 3.6 collective-permute-done.9
  653.0 4.5 collective-permute-start.10
  658.9 4.8 collective-permute-done.11
  664.1 1.5 fusion.10
  666.0 2.7 collective-permute-start.12
  668.7 1.9 collective-permute-start.13
  670.7 1.6 reshape.53
  672.3 2.3 collective-permute-done.13
  674.7 3.1 collective-permute-start.14
  677.8 1.5 collective-permute-start.15
  679.3 1.9 copy_dynamic-update-slice_fusion.1
  681.2 2.8 collective-permute-done.15
  684.3 3.0 add_convert_fusion
  689.0 1.3 copy-done.2
  691.1 1.4 copy-done.3
  693.6 105.8 %psum.31 = f32[16,32]{1,0:T(8,128)S(1)} all-reduce(f32[16,32]{1,0:T(8,128)S(1)} %convert_reduce_fusion), channel_id=1, replica_groups=mesh['row'=16,'col'=32] {'row','col'}, use_global_device_ids=true, to_apply=%region_5.6 | all-reduce | flops 512 | bytes 4096 | tf_op jit(solution)/shard_map/psum | solution.py:116
  799.4 5.4 fusion.29
  804.9 448.7 %all-reduce.5.cloned.1.call-done = f32[16,32,32]{1,2,0:T(8,128)} async-done(((f32[16,32,32]{1,2,0:T(8,128)}), f32[16,32,32]{1,2,0:T(8,128)}) %all-reduce.5.cloned.1.call-update) | async-done | bytes 65552 | tf_op jit(solution)/shard_map/psum | solution.py:116
  1253.6 6.1 fusion
  1262.1 4.9 collective-permute-start.16
  1267.0 1.9 collective-permute-start.17
  1269.2 2.9 collective-permute-done.17
  1272.1 4.5 collective-permute-start.18
  1278.3 4.2 collective-permute-done.19
  (167 shorter events, 26.7 us)
Async XLA Ops:
  7.2 13.1 %copy-start.35 = (f32[2,256]{1,0:T(2,128)S(1)}, f32[2,256]{1,0:T(2,128)}, u32[]{:S(2)}) copy-start(f32[2,256]{1,0:T(2,128)} %param.20) | copy-start | bytes 6148
  7.2 13.7 %copy-start.32 = (f32[2,1024]{1,0:T(2,128)S(1)}, f32[2,1024]{1,0:T(2,128)}, u32[]{:S(2)}) copy-start(f32[2,1024]{1,0:T(2,128)} %param.18) | copy-start | bytes 24580
  7.2 14.3 %copy-start.14 = (f32[2,3,3,1024]{3,0,2,1:T(2,128)S(1)}, f32[2,3,3,1024]{3,0,2,1:T(2,128)}, u32[]{:S(2)}) copy-start(f32[2,3,3,1024]{3,0,2,1:T(2,128)} %param.17) | copy-start | bytes 221188
  7.2 14.4 %copy-start.9 = (f32[2,5,5,768]{3,0,2,1:T(2,128)S(1)}, f32[2,5,5,768]{3,0,2,1:T(2,128)}, u32[]{:S(2)}) copy-start(f32[2,5,5,768]{3,0,2,1:T(2,128)} %param.22) | copy-start | bytes 460804
  7.2 625.4 %all-reduce.3.cloned.1.call-start = ((), (), s32[]{:S(2)}) async-start(), calls=%async_computation | async-start | bytes 524288 | tf_op jit(solution)/shard_map/psum | solution.py:116
  8.6 13.8 %copy-start.36 = (f32[2,256]{1,0:T(2,128)S(1)}, f32[2,256]{1,0:T(2,128)}, u32[]{:S(2)}) copy-start(f32[2,256]{1,0:T(2,128)} %param.25) | copy-start | bytes 6148
  10.1 12.8 collective-permute-start
  14.7 8.2 collective-permute-start.1
  23.0 8.6 copy-start.42
  23.0 8.6 copy-start.45
  23.1 3.9 collective-permute-start.2
  24.9 6.3 collective-permute-start.3
  33.1 6.6 copy-start.10
  34.1 7.9 collective-permute-start.4
  37.8 6.1 collective-permute-start.5
  44.0 9.3 collective-permute-start.6
  50.0 6.2 collective-permute-start.7
  53.2 3.4 copy-start.19
  53.2 3.4 copy-start.20
  53.2 3.4 copy-start.21
  53.2 3.4 copy-start.22
  53.2 3.4 copy-start.23
  53.2 3.4 copy-start.24
  53.3 3.4 copy-start.25
  53.3 3.4 copy-start.26
  53.3 3.4 copy-start.27
  53.3 3.4 copy-start.28
  182.4 1071.2 %all-reduce.5.cloned.1.call-start = ((), (), s32[]{:S(2)}) async-start(), calls=%async_computation.1 | async-start | bytes 524288 | tf_op jit(solution)/shard_map/psum | solution.py:116
  642.0 16.8 %copy-start.8 = (f32[5,5,768]{2,1,0:T(8,128)S(1)}, f32[5,5,768]{2,1,0:T(8,128)}, u32[]{:S(2)}) copy-start(f32[5,5,768]{2,1,0:T(8,128)} %get-tuple-element.118) | copy-start | bytes 230404
  642.4 7.0 collective-permute-start.8
  647.3 5.6 collective-permute-start.9
  649.3 14.8 %copy-start.33 = (f32[1,1024]{1,0:T(1,128)S(1)}, f32[1,1024]{1,0:T(1,128)}, u32[]{:S(2)}) copy-start(f32[1,1024]{1,0:T(1,128)} %get-tuple-element.108) | copy-start | bytes 12292
  649.3 14.8 %copy-start.38 = (f32[1,256]{1,0:T(1,128)S(1)}, f32[1,256]{1,0:T(1,128)}, u32[]{:S(2)}) copy-start(f32[1,256]{1,0:T(1,128)} %get-tuple-element.114) | copy-start | bytes 3076
  649.3 14.8 %copy-start.43 = (bf16[2,1024,256]{2,1,0:T(8,128)(2,1)S(1)}, bf16[2,1024,256]{2,1,0:T(8,128)(2,1)}, u32[]{:S(2)}) copy-start(bf16[2,1024,256]{2,1,0:T(8,128)(2,1)} %param.19) | copy-start | bytes 3145732
  653.0 6.0 collective-permute-start.10
  657.5 6.3 collective-permute-start.11
  665.6 5.0 copy-start.12
  666.0 6.3 collective-permute-start.12
  668.7 5.9 collective-permute-start.13
  674.7 6.6 collective-permute-start.14
  677.8 6.2 collective-permute-start.15
  1259.8 9.2 copy-start.40
  1261.8 21.8 %copy-start.46 = (f32[4]{0:T(128)S(1)}, f32[4]{0:T(128)}, u32[]{:S(2)}) copy-start(f32[4]{0:T(128)} %param.27) | copy-start | bytes 52
  1262.0 22.4 %copy-start.4 = (bf16[8,32,256]{2,1,0:T(8,128)(2,1)}, bf16[8,32,256]{2,1,0:T(8,128)(2,1)S(1)}, u32[]{:S(2)}) copy-start(bf16[8,32,256]{2,1,0:T(8,128)(2,1)S(1)} %fusion.9) | copy-start | bytes 393220
  1262.1 7.1 collective-permute-start.16
  1267.0 5.1 collective-permute-start.17
  1272.1 6.2 collective-permute-start.18
  1276.6 5.9 collective-permute-start.19
  (21 other events, 49.9 us)
Sparse Core Ops, SparseCore 0:
  182.6 449.9 all-reduce.2
  805.0 448.5 all-reduce.4
where the time goes:
time: 1290 us
  waiting for transfers between devices  929 us (72%)
  blocking collectives  217 us (17%)
  starting transfers between devices  60.7 us (5%)
  matrix products  35 us (3%)
  local copies, waits for them, and re-layouts  26.6 us (2%)
  between operations  15.2 us (1%)
    psum x2, waiting for transfers between devices, local(): kv_all, key_all = lax.psum((kv_local, key_local), ('row', 'col'))  899 us
    psum x2, blocking collectives, local(): kv_all, key_all = lax.psum((kv_local, key_local), ('row', 'col'))  217 us
    ppermute x10, starting transfers between devices, with_halo(): lax.ppermute(tail, axis, [(i, (i + 1) % count) for i in range(ends)])  40.8 us
    ppermute x10, waiting for transfers between devices, with_halo(): lax.ppermute(head, axis, [((i + 1) % count, i) for i in range(ends)])  29.7 us
  transfers between devices with their start and end apart: 22, of which 11 were waited for; matrix products, arithmetic and copies ran while one was open for 1% of the time, Pallas kernels for 0%

commit v1 on v0

v1 whole, which is shorter than its diff:
```python
import functools

import jax
import jax.numpy as jnp
from jax import lax
from jax.experimental import pallas as pl
from jax.experimental.pallas import tpu as pltpu
from jax.sharding import PartitionSpec as P

MESH = pl.DeviceIdType.MESH
F32 = jnp.float32
BF16 = jnp.bfloat16
ROWS = 8
COLS = 32
PITCH = 40
WIDTH = 256
EXPANDED = 1024
CHUNK = 256
HD = 32
HEADS = 8
HALOS = (3, 1)


def spot():
    return lax.axis_index("row"), lax.axis_index("col")


def beside(dr, dc):
    r, c = spot()
    return lax.rem(r + 16 + dr, 16), lax.rem(c + 32 + dc, 32)


def far_first(k, half):
    return half + (1 - 2 * lax.rem(k, 2)) * ((k + 1) // 2)


def plane_of(r, c):
    return r * 2 + lax.rem(c, 2)


def plane_peer(k):
    r, c = spot()
    dx = far_first(k // 8, 2)
    dy = far_first(lax.rem(k // 2, 4), 2)
    dk = 1 - lax.rem(k, 2)
    x = lax.rem(r // 4 + dx, 4)
    y = lax.rem(lax.rem(c, 2) * 2 + lax.rem(r // 2, 2) + dy, 4)
    core = lax.rem(r + dk, 2)
    return x * 4 + lax.rem(y, 2) * 2 + core, (c // 2) * 2 + y // 2


def depth_peer(k):
    r, c = spot()
    z = lax.rem(c // 2 + far_first(k, 8), 16)
    return r, z * 2 + lax.rem(c, 2)


AROUND = [(-1, 0), (1, 0), (0, -1), (0, 1), (-1, -1), (-1, 1), (1, -1), (1, 1)]


def each(count, body):
    def step(k, carry):
        body(k)
        return carry

    lax.fori_loop(0, count, step, 0)


def enter():
    barrier = pltpu.get_barrier_semaphore()

    def tell(device):
        pl.semaphore_signal(barrier, inc=1, device_id=device, device_id_type=MESH)

    each(15, lambda k: tell(depth_peer(k)))
    each(31, lambda k: tell(plane_peer(k)))
    for dr, dc in AROUND:
        tell(beside(dr, dc))


def entered():
    pl.semaphore_wait(pltpu.get_barrier_semaphore(), 15 + 31 + 8)


def dot(a, b):
    return jnp.dot(a, b, preferred_element_type=F32)


def gate(v):
    return v * jnp.minimum(jnp.maximum(v + 3.0, 0.0), 6.0)


def inside(rows, halo, lanes):
    r, c = spot()
    at = lax.broadcasted_iota(jnp.int32, (rows * PITCH, lanes), 0)
    row = at // PITCH
    col = at - row * PITCH
    row = row + (r * ROWS - halo)
    col = col + (c * COLS - halo)
    ok = (row >= 0) & (row < 128) & (col >= 0) & (col < 1024)
    return jnp.where(ok, 1.0, 0.0).astype(F32)


def pack(tile, left, right, packed, wide):
    for r in range(ROWS):
        row = tile(r)
        packed[0, 4 * r : 4 * r + 4, :wide] = row[0:4]
        packed[1, 4 * r : 4 * r + 4, :wide] = row[COLS - 4 : COLS]
    left[...] = packed[0, :, :wide].astype(BF16)
    right[...] = packed[1, :, :wide].astype(BF16)


def trade(tile, left, right, halo, across, sides, corners, send, recv):
    low = tile.at[pl.ds(ROWS - halo, halo)]
    high = tile.at[pl.ds(0, halo)]
    top = pl.ds(0, 16)
    bottom = pl.ds(16, 16)
    plan = [
        ((1, 0), low, across.at[0]),
        ((-1, 0), high, across.at[1]),
        ((0, 1), right, sides.at[0]),
        ((0, -1), left, sides.at[1]),
        ((1, 1), right.at[bottom], corners.at[0]),
        ((1, -1), left.at[bottom], corners.at[1]),
        ((-1, 1), right.at[top], corners.at[2]),
        ((-1, -1), left.at[top], corners.at[3]),
    ]
    return [
        pltpu.make_async_remote_copy(
            src_ref=src,
            dst_ref=dst,
            send_sem=send.at[i],
            recv_sem=recv.at[i],
            device_id=beside(*where),
            device_id_type=MESH,
        )
        for i, (where, src, dst) in enumerate(plan)
    ]


def assemble(out, tile, halo, across, sides, corners):
    wide = out.shape[1]
    skip = 4 - halo
    ends = halo + COLS

    def put(row, col, value):
        start = row * PITCH + col
        out[start : start + value.shape[0], :] = value

    for r in range(ROWS):
        put(halo + r, halo, tile[r].astype(F32))
    for r in range(halo):
        put(r, halo, across[0, r].astype(F32))
        put(halo + ROWS + r, halo, across[1, r].astype(F32))
    west = sides[0].astype(F32)
    east = sides[1].astype(F32)
    for r in range(ROWS):
        put(halo + r, 0, west[4 * r + skip : 4 * r + 4])
        put(halo + r, ends, east[4 * r : 4 * r + halo])
    nw, ne, sw, se = [corners[i].astype(F32) for i in range(4)]
    for r in range(halo):
        low = 4 * (r + skip)
        put(r, 0, nw[low + skip : low + 4])
        put(r, ends, ne[low : low + halo])
        put(halo + ROWS + r, 0, sw[4 * r + skip : 4 * r + 4])
        put(halo + ROWS + r, ends, se[4 * r : 4 * r + halo])


def prepare(s, qkv_weight, agg_depth, agg_group, qkv_w, agg_w, grp_w, stack):
    i = lax.broadcasted_iota(jnp.int32, (3 * WIDTH, 3 * WIDTH), 0)
    j = lax.broadcasted_iota(jnp.int32, (3 * WIDTH, 3 * WIDTH), 1)
    kind = j // WIDTH
    head = (j - kind * WIDTH) // HD
    lane = j - (j // HD) * HD
    order = jnp.where(i == head * (3 * HD) + kind * HD + lane, 1.0, 0.0).astype(BF16)
    qkv_w[s] = dot(qkv_weight[s], order).astype(BF16)
    stack[...] = jnp.zeros_like(stack)
    for a in range(5):
        full = agg_depth[s, a]
        high = full.astype(BF16).astype(F32)
        rest = full - high
        mid = rest.astype(BF16).astype(F32)
        stack[8 * a : 8 * a + 5] = high
        stack[48 + 8 * a : 48 + 8 * a + 5] = mid
        stack[96 + 8 * a : 96 + 8 * a + 5] = rest - mid
    moved = dot(stack[...].astype(BF16), order)
    agg_w[s] = moved[0:48] + moved[48:96] + moved[96:144]
    i = lax.broadcasted_iota(jnp.int32, (HD, WIDTH), 0)
    j = lax.broadcasted_iota(jnp.int32, (HD, WIDTH), 1)
    spread = jnp.where(i == j - (j // HD) * HD, 1.0, 0.0).astype(BF16)
    i = lax.broadcasted_iota(jnp.int32, (WIDTH, WIDTH), 0)
    j = lax.broadcasted_iota(jnp.int32, (WIDTH, WIDTH), 1)
    same = i // HD == j // HD
    for t in range(3):
        rows = jnp.concatenate([agg_group[s, 3 * h + t] for h in range(HEADS)], axis=0)
        grp_w[s, t] = jnp.where(same, dot(rows, spread), 0.0).astype(BF16)


def kernel(
    features,
    expand_weight,
    expand_bias,
    depth_weight,
    depth_bias,
    project_weight,
    project_bias,
    qkv_weight,
    agg_depth,
    agg_group,
    output_weight,
    output_bias,
    head_weight,
    head_bias,
    out_map,
    out_boxes,
    xp,
    xb,
    edge3,
    edge2,
    hidden,
    spread,
    acc,
    qkv,
    scaled,
    center,
    mixed,
    joined,
    qkv_w,
    agg_w,
    grp_w,
    stack,
    head_w,
    packed,
    lefts,
    rights,
    f_left,
    f_right,
    tile,
    f_across,
    f_sides,
    f_corners,
    across3,
    across1,
    sides,
    corners,
    part,
    got,
    mine,
    deep,
    total,
    whole,
    table,
    keys,
    hs_send,
    hs_recv,
    ar_send,
    ar_recv,
):
    enter()
    pack(
        lambda r: features[r].astype(F32), f_left, f_right, packed, WIDTH
    )
    for s in range(2):
        prepare(s, qkv_weight, agg_depth, agg_group, qkv_w, agg_w, grp_w, stack)
    head_w[...] = jnp.zeros_like(head_w)
    for a in range(3):
        for b in range(3):
            at = 8 * (3 * a + b)
            head_w[at : at + 4] = head_weight[a, b].astype(F32)
    edge3[...] = inside(14, 3, 128) * (1.0 / 6.0)
    edge2[...] = inside(12, 2, 128)
    xp[...] = jnp.zeros_like(xp)
    joined[...] = jnp.zeros_like(joined)
    part[...] = jnp.zeros_like(part)
    entered()

    first = trade(
        features, f_left, f_right, 3, f_across, f_sides, f_corners, hs_send.at[2], hs_recv.at[2]
    )
    for copy in first:
        copy.start()
    for copy in first:
        copy.wait()
    assemble(xp, features, 3, f_across, f_sides, f_corners)
    xb[...] = xp[...].astype(BF16)

    for s in range(2):
        halo = HALOS[s]
        acc[...] = jnp.zeros_like(acc)

        def expand(c, carry, s=s):
            wide = pl.ds(pl.multiple_of(c * CHUNK, CHUNK), CHUNK)
            value = gate(dot(xb[...], expand_weight[s, :, wide]) + expand_bias[s : s + 1, wide])
            for l in range(CHUNK // 128):
                hidden[:, 128 * l : 128 * l + 128] = (
                    value[:, 128 * l : 128 * l + 128] * edge3[...]
                )
            for l in range(CHUNK // 128):
                here = slice(128 * l, 128 * l + 128)
                lanes = pl.ds(pl.multiple_of(c * CHUNK + 128 * l, 128), 128)
                taps = [
                    [depth_weight[s, a, b : b + 1, lanes] for b in range(3)] for a in range(3)
                ]
                bias = depth_bias[s : s + 1, lanes]
                for pair in range(6):
                    done = []
                    for r in (2 * pair, 2 * pair + 1):
                        rows = [
                            hidden[PITCH * (r + a) : PITCH * (r + a) + PITCH, here]
                            for a in range(3)
                        ]
                        cols = [
                            rows[0] * taps[0][b] + rows[1] * taps[1][b] + rows[2] * taps[2][b]
                            for b in range(3)
                        ]
                        value = (
                            cols[0]
                            + pltpu.roll(cols[1], PITCH - 1, 0)
                            + pltpu.roll(cols[2], PITCH - 2, 0)
                            + bias
                        )
                        done.append(gate(value) * (1.0 / 6.0))
                    spread[2 * PITCH * pair : 2 * PITCH * (pair + 1), here] = jnp.concatenate(
                        done, axis=0
                    ).astype(BF16)
            acc[...] += dot(spread[...], project_weight[s, wide, :])
            return carry

        lax.fori_loop(0, EXPANDED // CHUNK, expand, 0)
        bias = project_bias[s : s + 1]
        for r in range(12):
            here = slice(PITCH * r, PITCH * r + PITCH)
            base = xp[PITCH * (r + 1) : PITCH * (r + 2)]
            value = acc[here] + pltpu.roll(base, PITCH - 1, 0) + bias
            for l in range(WIDTH // 128):
                lanes = slice(128 * l, 128 * l + 128)
                mixed[here, lanes] = value[:, lanes] * edge2[here]
        qkv[...] = dot(mixed[...].astype(BF16), qkv_w[s])

        def taps5(l, carry, s=s):
            lanes = pl.ds(pl.multiple_of(l * 128, 128), 128)
            for r in range(ROWS):
                cols = [None] * 5
                for a in range(5):
                    row = qkv[PITCH * (r + a) : PITCH * (r + a) + PITCH, lanes]
                    for b in range(5):
                        term = row * agg_w[s, 8 * a + b : 8 * a + b + 1, lanes]
                        cols[b] = term if a == 0 else cols[b] + term
                value = cols[0]
                for b in range(1, 5):
                    value = value + pltpu.roll(cols[b], PITCH - b, 0)
                scaled[COLS * r : COLS * r + COLS, lanes] = value[0:COLS].astype(BF16)
                near = pltpu.roll(qkv[PITCH * (r + 2) : PITCH * (r + 3), lanes], PITCH - 2, 0)
                center[COLS * r : COLS * r + COLS, lanes] = near[0:COLS].astype(BF16)
            return carry

        def kind(t):
            lanes = slice(WIDTH * t, WIDTH * t + WIDTH)
            return [center[:, lanes], dot(scaled[:, lanes], grp_w[s, t]).astype(BF16)]

        lax.fori_loop(2, 6, taps5, 0)
        lane = lax.broadcasted_iota(jnp.int32, (HD, 128), 1) // HD
        ones = jnp.ones((16, ROWS * COLS), BF16)
        for branch, (k, v) in enumerate(zip(kind(1), kind(2))):
            k = jnp.maximum(k, jnp.zeros_like(k))
            outer = lax.dot_general(k, v, (((0,), (0,)), ((), ())), preferred_element_type=F32)
            count = dot(ones, k)
            for g in range(2):
                group = 2 * branch + g
                lanes = slice(128 * g, 128 * g + 128)
                fold = jnp.zeros((HD, 128), F32)
                for h in range(4):
                    low = 128 * g + HD * h
                    fold = jnp.where(lane == h, outer[low : low + HD, lanes], fold)
                for p in range(8):
                    part[s, 8 * group + p, 0:4, :] = fold[4 * p : 4 * p + 4]
                part[s, group, 4:5, :] = count[0:1, lanes]

        me = plane_of(*spot())
        depth = spot()[1] // 2

        def remote(src, dst, stage, device):
            return pltpu.make_async_remote_copy(
                src_ref=src,
                dst_ref=dst,
                send_sem=ar_send.at[s, stage],
                recv_sem=ar_recv.at[s, stage],
                device_id=device,
                device_id_type=MESH,
            )

        def send1(k, s=s):
            device = plane_peer(k)
            remote(part.at[s, plane_of(*device)], got.at[s, me], 0, device).start()

        def send2(k, s=s):
            remote(mine.at[s], deep.at[s, depth], 1, depth_peer(k)).start()

        def send3(k, s=s):
            remote(total.at[s], whole.at[s, me], 2, plane_peer(k)).start()

        def arrived(buffer, count, stage, s=s):
            view = buffer.at[s, pl.ds(0, count)]
            pltpu.make_async_copy(view, view, ar_recv.at[s, stage]).wait()

        def sent(buffer, count, stage, s=s):
            view = buffer.at[s, pl.ds(0, count)]
            pltpu.make_async_copy(view, view, ar_send.at[s, stage]).wait()

        each(31, send1)
        got[s, me] = part[s, me]

        lax.fori_loop(0, 2, taps5, 0)
        near, far = kind(0)
        for r in range(ROWS):
            here = slice(COLS * r, COLS * r + COLS)
            value = pltpu.roll(mixed[PITCH * (r + 2) : PITCH * (r + 3)], PITCH - 2, 0)
            tile[s, r, :, 0:WIDTH] = value[0:COLS].astype(BF16)
            tile[s, r, :, WIDTH : 2 * WIDTH] = jnp.maximum(near[here], jnp.zeros_like(near[here]))
            tile[s, r, :, 2 * WIDTH :] = jnp.maximum(far[here], jnp.zeros_like(far[here]))
        pack(
            lambda r, s=s: tile[s, r].astype(F32), lefts.at[s], rights.at[s], packed, 3 * WIDTH
        )
        across = across3 if halo == 3 else across1
        swap = trade(
            tile.at[s],
            lefts.at[s],
            rights.at[s],
            halo,
            across,
            sides.at[s],
            corners.at[s],
            hs_send.at[s],
            hs_recv.at[s],
        )

        arrived(got, 31, 0)
        mine[s] = jnp.sum(got[s], axis=0)
        each(15, send2)
        deep[s, depth] = mine[s]
        for copy in swap:
            copy.start()
        for copy in swap:
            copy.wait()
        area = (ROWS + 2 * halo) * PITCH
        assemble(joined.at[pl.ds(0, area)], tile.at[s], halo, across, sides.at[s], corners.at[s])
        arrived(deep, 15, 1)
        total[s] = jnp.sum(deep[s], axis=0)
        each(31, send3)
        whole[s, me] = total[s]
        arrived(whole, 31, 2)
        sent(got, 31, 0)
        sent(deep, 15, 1)
        sent(whole, 31, 2)

        for p in range(32):
            table[4 * p : 4 * p + 4, :] = whole[s, p, 0:4, :]
        i = lax.broadcasted_iota(jnp.int32, (WIDTH, WIDTH), 0)
        j = lax.broadcasted_iota(jnp.int32, (WIDTH, WIDTH), 1)
        same = i // HD == j // HD
        ones = jnp.where(same, 1.0, 0.0).astype(BF16)
        attended = []
        for branch in range(2):
            blocks = []
            for g in range(2):
                group = 2 * branch + g
                block = table[HD * group : HD * group + HD]
                blocks.append(jnp.concatenate([block] * 4, axis=0))
                keys[0:1, 128 * g : 128 * g + 128] = whole[s, group, 4:5, :]
            numer_w = jnp.where(
                same, jnp.concatenate([jnp.concatenate([b, b], axis=1) for b in blocks], axis=0), 0.0
            )
            key_row = jnp.broadcast_to(keys[0:1, :], (WIDTH, WIDTH))
            denom_w = dot(jnp.where(i == j, key_row, 0.0).astype(BF16), ones)
            q = joined[0:area, WIDTH * (1 + branch) : WIDTH * (2 + branch)].astype(BF16)
            numer = dot(q, numer_w.astype(BF16))
            denom = dot(q, denom_w.astype(BF16))
            attended.append((numer / (denom + 1e-06)).astype(BF16))
        value = (
            joined[0:area, 0:WIDTH]
            + dot(attended[0], output_weight[s, 0:WIDTH])
            + dot(attended[1], output_weight[s, WIDTH:])
            + output_bias[s : s + 1]
        )
        xp[0:area] = value
        xb[0:area] = value.astype(BF16)

    for r in range(ROWS):
        start = PITCH * (r + 1) + 1
        out_map[r] = xp[start : start + COLS].astype(BF16)
    area = 10 * PITCH
    on_map = inside(10, 1, 128)
    final = jnp.concatenate(
        [
            (xp[0:area, 128 * l : 128 * l + 128] * on_map).astype(BF16)
            for l in range(WIDTH // 128)
        ],
        axis=1,
    )
    final = jnp.concatenate([final, jnp.zeros((512 - area, WIDTH), BF16)], axis=0)
    taps = lax.dot_general(
        head_w[...].astype(BF16), final, (((1,), (1,)), ((), ())), preferred_element_type=F32
    )
    boxes = jnp.zeros((8, 512), F32)
    for a in range(3):
        for b in range(3):
            at = 8 * (3 * a + b)
            shift = PITCH * a + b
            term = taps[at : at + 8]
            boxes = boxes + (term if shift == 0 else pltpu.roll(term, 512 - shift, 1))
    for r in range(ROWS):
        row = boxes if r == 0 else pltpu.roll(boxes, 512 - PITCH * r, 1)
        for o in range(4):
            out_boxes[o, r : r + 1, :] = row[o : o + 1, 0:COLS] + head_bias[o]


def local(*args):
    dma = pltpu.SemaphoreType.DMA
    vmem = pltpu.VMEM
    area = 14 * PITCH
    inner = 12 * PITCH
    wide = 3 * WIDTH
    scratch = [
        vmem((area, WIDTH), F32),
        vmem((area, WIDTH), BF16),
        vmem((area, 128), F32),
        vmem((inner, 128), F32),
        vmem((area, CHUNK), F32),
        vmem((inner, CHUNK), BF16),
        vmem((inner, WIDTH), F32),
        vmem((inner, wide), F32),
        vmem((ROWS * COLS, wide), BF16),
        vmem((ROWS * COLS, wide), BF16),
        vmem((inner, WIDTH), F32),
        vmem((area, wide), F32),
        vmem((2, WIDTH, wide), BF16),
        vmem((2, 48, wide), F32),
        vmem((2, 3, WIDTH, WIDTH), BF16),
        vmem((144, wide), F32),
        vmem((72, WIDTH), F32),
        vmem((2, 32, wide), F32),
        vmem((2, 32, wide), BF16),
        vmem((2, 32, wide), BF16),
        vmem((32, WIDTH), BF16),
        vmem((32, WIDTH), BF16),
        vmem((2, ROWS, COLS, wide), BF16),
        vmem((2, 3, COLS, WIDTH), BF16),
        vmem((2, 32, WIDTH), BF16),
        vmem((4, 16, WIDTH), BF16),
        vmem((2, 3, COLS, wide), BF16),
        vmem((2, 1, COLS, wide), BF16),
        vmem((2, 2, 32, wide), BF16),
        vmem((2, 4, 16, wide), BF16),
        vmem((2, 32, 5, 128), F32),
        vmem((2, 32, 5, 128), F32),
        vmem((2, 5, 128), F32),
        vmem((2, 16, 5, 128), F32),
        vmem((2, 5, 128), F32),
        vmem((2, 32, 5, 128), F32),
        vmem((128, 128), F32),
        vmem((8, WIDTH), F32),
        dma((3, 8)),
        dma((3, 8)),
        dma((2, 3)),
        dma((2, 3)),
    ]
    in_vmem = pl.BlockSpec(memory_space=pltpu.VMEM)
    return pl.pallas_call(
        kernel,
        out_shape=(
            jax.ShapeDtypeStruct((ROWS, COLS, WIDTH), BF16),
            jax.ShapeDtypeStruct((4, ROWS, COLS), F32),
        ),
        in_specs=[in_vmem] * 13 + [pl.BlockSpec(memory_space=pltpu.SMEM)],
        out_specs=(in_vmem, in_vmem),
        scratch_shapes=scratch,
        compiler_params=pltpu.CompilerParams(
            collective_id=0, has_side_effects=True, vmem_limit_bytes=48 * 1024 * 1024
        ),
    )(*args)


def solution(mesh):
    return jax.shard_map(
        local,
        mesh=mesh,
        in_specs=(P("row", "col", None),) + (P(),) * 13,
        out_specs=(P("row", "col", None), P(None, "row", "col")),
        check_vma=False,
    )
```

time: 1290 us -> 84.1 us (0.07)
  waiting for transfers between devices: 929 us -> 0 us
  blocking collectives: 217 us -> 0 us
  Pallas kernels: 0 us -> 74.3 us
  starting transfers between devices: 60.7 us -> 0 us
  matrix products: 35 us -> 0 us
  local copies, waits for them, and re-layouts: 26.6 us -> 8.73 us
  between operations: 15.2 us -> 0.77 us
    psum x2 -> x0, waiting for transfers between devices: 899 us -> none  [local(): kv_all, key_all = lax.psum((kv_local, key_local), ('row', 'col'))]
    psum x2 -> x0, blocking collectives: 217 us -> none  [local(): kv_all, key_all = lax.psum((kv_local, key_local), ('row', 'col'))]
    pallas_call x0 -> x1, Pallas kernels: none -> 74.3 us  [local(): pl.pallas_call(kernel, out_shape=(jax.ShapeDtypeStruct((ROWS, COLS, WIDTH...]
    ppermute x20 -> x0, starting transfers between devices: 60.7 us -> none  [the longest x10 40.8 us: with_halo(): lax.ppermute(tail, axis, [(i, (i + 1) % count) for i in range(ends)])]
    dot_general x25 -> x0, matrix products: 35 us -> none  [the longest x2 12.2 us: local(): jnp.einsum('rchd,hde->rche', queries, kv_all, precision=lax.Precision.HIG...]
    ppermute x20 -> x0, waiting for transfers between devices: 29.7 us -> none  [the longest x10 29.7 us: with_halo(): lax.ppermute(head, axis, [((i + 1) % count, i) for i in range(ends)])]
  transfers between devices with their start and end apart: 22 -> 0, of which waited for: 11 -> 0; matrix products, arithmetic and copies ran while one was open for 1% -> 0% of each run, Pallas kernels for 0% -> 0%
where the time goes in v1:
time: 84.1 us; the launch traced here: 83.8 us
  Pallas kernels  74.3 us (88%)
  local copies, waits for them, and re-layouts  8.73 us (10%)
    pallas_call x1, Pallas kernels, local(): pl.pallas_call(kernel, out_shape=(jax.ShapeDtypeStruct((ROWS, COLS, WIDTH...  74.3 us
    unnamed x28, local copies, waits for them, and re-layouts  8.73 us

profile of v1, /device:TPU:1, one launch (start us, length us, event | category | flops | bytes accessed | tf_op | source)
XLA Modules:
  0.0 83.8 jit_solution(14258708140253939821)
XLA Ops:
  0.6 0.0 copy-start.3
  0.6 1.0 %copy.16.depth_weight = f32[2,3,3,1024]{3,2,1,0:T(4,128)S(1)} copy(f32[2,3,3,1024]{3,0,2,1:T(2,128)} %param.17) | data formatting | bytes 147456 | tf_op args[3]
  1.6 0.0 copy-start.6
  1.6 0.0 copy-start.7
  1.7 0.0 copy-start.8
  1.7 0.0 copy-start.9
  1.7 0.0 copy-start.10
  1.7 0.0 copy-start.11
  1.7 1.0 %copy.17.agg_depth = f32[2,5,5,768]{3,2,1,0:T(8,128)S(1)} copy(f32[2,5,5,768]{3,0,2,1:T(2,128)} %param.22) | data formatting | bytes 307200 | tf_op args[8]
  2.7 0.0 copy-done.3
  2.7 0.0 copy-done.6
  2.7 0.0 copy-done.7
  2.7 0.0 copy-done.8
  2.7 0.0 copy-done.9
  2.7 0.0 copy-done.10
  2.7 0.0 copy-done.11
  2.7 0.0 copy-start
  2.8 1.2 %copy-done = bf16[2,256,1024]{2,1,0:T(8,128)(2,1)S(1)} copy-done((bf16[2,256,1024]{2,1,0:T(8,128)(2,1)S(1)}, bf16[2,256,1024]{2,1,0:T(8,128)(2,1)}, u32[]{:S(2)}) %copy-start) | copy-done | bytes 1048600
  4.0 0.0 copy-start.1
  4.0 1.2 %copy-done.1 = bf16[2,1024,256]{2,1,0:T(8,128)(2,1)S(1)} copy-done((bf16[2,1024,256]{2,1,0:T(8,128)(2,1)S(1)}, bf16[2,1024,256]{2,1,0:T(8,128)(2,1)}, u32[]{:S(2)}) %copy-start.1) | copy-done | bytes 1048600
  5.2 0.0 copy-start.2
  5.2 1.1 %copy-done.2 = bf16[2,256,768]{2,1,0:T(8,128)(2,1)S(1)} copy-done((bf16[2,256,768]{2,1,0:T(8,128)(2,1)S(1)}, bf16[2,256,768]{2,1,0:T(8,128)(2,1)}, u32[]{:S(2)}) %copy-start.2) | copy-done | bytes 786456
  6.3 0.0 copy-start.4
  6.3 1.0 %copy-done.4 = bf16[2,24,32,32]{3,2,1,0:T(8,128)(2,1)S(1)} copy-done((bf16[2,24,32,32]{3,2,1,0:T(8,128)(2,1)S(1)}, bf16[2,24,32,32]{3,2,1,0:T(8,128)(2,1)}, u32[]{:S(2)}) %copy-start.4) | copy-done | bytes 98328
  7.3 0.0 copy-start.5
  7.3 0.9 %copy-done.5 = bf16[8,32,256]{2,1,0:T(8,128)(2,1)S(1)} copy-done((bf16[8,32,256]{2,1,0:T(8,128)(2,1)S(1)}, bf16[8,32,256]{2,1,0:T(8,128)(2,1)}, u32[]{:S(2)}) %copy-start.5) | copy-done | bytes 131096
  8.2 74.3 %shard_map.149 = (bf16[8,32,256]{2,1,0:T(8,128)(2,1)S(1)}, f32[4,8,32]{2,1,0:T(8,128)S(1)}) custom-call(bf16[8,32,256]{2,1,0:T(8,128)(2,1)S(1)} %copy-done.5, bf16[2,256,1024]{2,1,0:T(8,128)(2,1)S(1)} %copy-done, f32[2,1024]{1,0:T(2,128)S(1)} %copy-done.7, f32[2,3,3,1024]{3,2,1,0:T(4,128)S(1)} %copy.16.depth_weight, f32[2,1024]{1,0:T(2,128)S(1)} %copy-done.8, ...), custom_call_target="tpu_custom_call" | custom-call | tf_op jit(solution)/shard_map/pallas_call | solution.py:568
  82.5 0.7 copy.20
  83.2 0.6 copy.21
Async XLA Ops:
  0.6 2.0 %copy-start.3 = (bf16[2,512,256]{2,1,0:T(8,128)(2,1)S(1)}, bf16[2,512,256]{2,1,0:T(8,128)(2,1)}, u32[]{:S(2)}) copy-start(bf16[2,512,256]{2,1,0:T(8,128)(2,1)} %output_weight.1) | copy-start | bytes 1572868
  1.6 1.1 %copy-start.6 = (bf16[3,3,4,256]{3,2,1,0:T(4,128)(2,1)S(1)}, bf16[3,3,4,256]{3,2,1,0:T(4,128)(2,1)}, u32[]{:S(2)}) copy-start(bf16[3,3,4,256]{3,2,1,0:T(4,128)(2,1)} %head_weight.1) | copy-start | bytes 55300
  1.6 1.1 %copy-start.7 = (f32[2,1024]{1,0:T(2,128)S(1)}, f32[2,1024]{1,0:T(2,128)}, u32[]{:S(2)}) copy-start(f32[2,1024]{1,0:T(2,128)} %expand_bias.1) | copy-start | bytes 24580
  1.7 1.1 %copy-start.8 = (f32[2,1024]{1,0:T(2,128)S(1)}, f32[2,1024]{1,0:T(2,128)}, u32[]{:S(2)}) copy-start(f32[2,1024]{1,0:T(2,128)} %depth_bias.1) | copy-start | bytes 24580
  1.7 1.1 %copy-start.9 = (f32[2,256]{1,0:T(2,128)S(1)}, f32[2,256]{1,0:T(2,128)}, u32[]{:S(2)}) copy-start(f32[2,256]{1,0:T(2,128)} %project_bias.1) | copy-start | bytes 6148
  1.7 1.0 %copy-start.10 = (f32[2,256]{1,0:T(2,128)S(1)}, f32[2,256]{1,0:T(2,128)}, u32[]{:S(2)}) copy-start(f32[2,256]{1,0:T(2,128)} %output_bias.1) | copy-start | bytes 6148
  1.7 1.0 %copy-start.11 = (f32[4]{0:T(128)S(1)}, f32[4]{0:T(128)}, u32[]{:S(2)}) copy-start(f32[4]{0:T(128)} %head_bias.1) | copy-start | bytes 52
  2.7 1.2 %copy-start = (bf16[2,256,1024]{2,1,0:T(8,128)(2,1)S(1)}, bf16[2,256,1024]{2,1,0:T(8,128)(2,1)}, u32[]{:S(2)}) copy-start(bf16[2,256,1024]{2,1,0:T(8,128)(2,1)} %expand_weight.1) | copy-start | bytes 3145732
  4.0 1.2 %copy-start.1 = (bf16[2,1024,256]{2,1,0:T(8,128)(2,1)S(1)}, bf16[2,1024,256]{2,1,0:T(8,128)(2,1)}, u32[]{:S(2)}) copy-start(bf16[2,1024,256]{2,1,0:T(8,128)(2,1)} %project_weight.1) | copy-start | bytes 3145732
  5.2 1.1 %copy-start.2 = (bf16[2,256,768]{2,1,0:T(8,128)(2,1)S(1)}, bf16[2,256,768]{2,1,0:T(8,128)(2,1)}, u32[]{:S(2)}) copy-start(bf16[2,256,768]{2,1,0:T(8,128)(2,1)} %qkv_weight.1) | copy-start | bytes 2359300
  6.3 1.0 %copy-start.4 = (bf16[2,24,32,32]{3,2,1,0:T(8,128)(2,1)S(1)}, bf16[2,24,32,32]{3,2,1,0:T(8,128)(2,1)}, u32[]{:S(2)}) copy-start(bf16[2,24,32,32]{3,2,1,0:T(8,128)(2,1)} %agg_group.1) | copy-start | bytes 294916
  7.3 0.9 %copy-start.5 = (bf16[8,32,256]{2,1,0:T(8,128)(2,1)S(1)}, bf16[8,32,256]{2,1,0:T(8,128)(2,1)}, u32[]{:S(2)}) copy-start(bf16[8,32,256]{2,1,0:T(8,128)(2,1)} %features.1) | copy-start | bytes 393220

commit v2 on v1

--- a/solution.py
+++ b/solution.py
@@ -66,20 +66,26 @@
     lax.fori_loop(0, count, step, 0)
 
 
+def along(dz):
+    r, c = spot()
+    return r, lax.rem(c // 2 + 16 + dz, 16) * 2 + lax.rem(c, 2)
+
+
+def tell(semaphore, device):
+    pl.semaphore_signal(semaphore, inc=1, device_id=device, device_id_type=MESH)
+
+
 def enter():
     barrier = pltpu.get_barrier_semaphore()
-
-    def tell(device):
-        pl.semaphore_signal(barrier, inc=1, device_id=device, device_id_type=MESH)
-
-    each(15, lambda k: tell(depth_peer(k)))
-    each(31, lambda k: tell(plane_peer(k)))
     for dr, dc in AROUND:
-        tell(beside(dr, dc))
+        tell(barrier, beside(dr, dc))
+    each(31, lambda k: tell(barrier, plane_peer(k)))
+    for dz in (1, -1):
+        tell(barrier, along(dz))
 
 
 def entered():
-    pl.semaphore_wait(pltpu.get_barrier_semaphore(), 15 + 31 + 8)
+    pl.semaphore_wait(pltpu.get_barrier_semaphore(), 8 + 31 + 2)
 
 
 def dot(a, b):
@@ -166,119 +172,135 @@
         put(halo + ROWS + r, ends, se[4 * r : 4 * r + halo])
 
 
-def prepare(s, qkv_weight, agg_depth, agg_group, qkv_w, agg_w, grp_w, stack):
+def prepare(qkv_weight, agg_depth, agg_group, qkv_w, agg_w, grp_w, stack):
     i = lax.broadcasted_iota(jnp.int32, (3 * WIDTH, 3 * WIDTH), 0)
     j = lax.broadcasted_iota(jnp.int32, (3 * WIDTH, 3 * WIDTH), 1)
     kind = j // WIDTH
     head = (j - kind * WIDTH) // HD
     lane = j - (j // HD) * HD
     order = jnp.where(i == head * (3 * HD) + kind * HD + lane, 1.0, 0.0).astype(BF16)
-    qkv_w[s] = dot(qkv_weight[s], order).astype(BF16)
     stack[...] = jnp.zeros_like(stack)
-    for a in range(5):
-        full = agg_depth[s, a]
-        high = full.astype(BF16).astype(F32)
-        rest = full - high
-        mid = rest.astype(BF16).astype(F32)
-        stack[8 * a : 8 * a + 5] = high
-        stack[48 + 8 * a : 48 + 8 * a + 5] = mid
-        stack[96 + 8 * a : 96 + 8 * a + 5] = rest - mid
-    moved = dot(stack[...].astype(BF16), order)
-    agg_w[s] = moved[0:48] + moved[48:96] + moved[96:144]
+    for s in range(2):
+        qkv_w[s] = dot(qkv_weight[s], order).astype(BF16)
+        for a in range(5):
+            for b in range(5):
+                at = 40 * s + 8 * a + b
+                stack[at : at + 1] = agg_depth[a, b, s : s + 1]
+    full = stack[...]
+    high = full.astype(BF16)
+    rest = full - high.astype(F32)
+    mid = rest.astype(BF16)
+    low = (rest - mid.astype(F32)).astype(BF16)
+    moved = dot(high, order) + dot(mid, order) + dot(low, order)
     i = lax.broadcasted_iota(jnp.int32, (HD, WIDTH), 0)
     j = lax.broadcasted_iota(jnp.int32, (HD, WIDTH), 1)
     spread = jnp.where(i == j - (j // HD) * HD, 1.0, 0.0).astype(BF16)
     i = lax.broadcasted_iota(jnp.int32, (WIDTH, WIDTH), 0)
     j = lax.broadcasted_iota(jnp.int32, (WIDTH, WIDTH), 1)
     same = i // HD == j // HD
-    for t in range(3):
-        rows = jnp.concatenate([agg_group[s, 3 * h + t] for h in range(HEADS)], axis=0)
-        grp_w[s, t] = jnp.where(same, dot(rows, spread), 0.0).astype(BF16)
-
-
-def kernel(
-    features,
-    expand_weight,
-    expand_bias,
-    depth_weight,
-    depth_bias,
-    project_weight,
-    project_bias,
-    qkv_weight,
-    agg_depth,
-    agg_group,
-    output_weight,
-    output_bias,
-    head_weight,
-    head_bias,
-    out_map,
-    out_boxes,
-    xp,
-    xb,
-    edge3,
-    edge2,
-    hidden,
-    spread,
-    acc,
-    qkv,
-    scaled,
-    center,
-    mixed,
-    joined,
-    qkv_w,
-    agg_w,
-    grp_w,
-    stack,
-    head_w,
-    packed,
-    lefts,
-    rights,
-    f_left,
-    f_right,
-    tile,
-    f_across,
-    f_sides,
-    f_corners,
-    across3,
-    across1,
-    sides,
-    corners,
-    part,
-    got,
-    mine,
-    deep,
-    total,
-    whole,
-    table,
-    keys,
-    hs_send,
-    hs_recv,
-    ar_send,
-    ar_recv,
-):
+    for s in range(2):
+        agg_w[s] = moved[40 * s : 40 * s + 40]
+        for t in range(3):
+            rows = jnp.concatenate([agg_group[s, 3 * h + t] for h in range(HEADS)], axis=0)
+            grp_w[s, t] = jnp.where(same, dot(rows, spread), 0.0).astype(BF16)
+
+
+def kernel(*refs):
+    given, (out_map, out_boxes), held = refs[:14], refs[14:16], refs[16:30]
+    (
+        features,
+        expand_weight,
+        expand_bias,
+        depth_weight,
+        depth_bias,
+        project_weight,
+        project_bias,
+        qkv_weight,
+        agg_depth,
+        agg_group,
+        output_weight,
+        output_bias,
+        head_weight,
+        head_bias,
+    ) = held
+    (
+        xp,
+        xb,
+        edge3,
+        edge2,
+        hidden,
+        spread,
+        acc,
+        qkv,
+        scaled,
+        center,
+        mixed,
+        joined,
+        qkv_w,
+        agg_w,
+        grp_w,
+        stack,
+        head_w,
+        packed,
+        lefts,
+        rights,
+        f_left,
+        f_right,
+        tile,
+        f_across,
+        f_sides,
+        f_corners,
+        across3,
+        across1,
+        sides,
+        corners,
+        part,
+        got,
+        mine,
+        deep,
+        total,
+        whole,
+        table,
+        keys,
+        hs_send,
+        hs_recv,
+        ar_send,
+        ar_recv,
+        ring,
+        load,
+    ) = refs[30:]
+    loads = [
+        pltpu.make_async_copy(src, dst, load.at[i]) for i, (src, dst) in enumerate(zip(given, held))
+    ]
+    for copy in loads:
+        copy.start()
     enter()
-    pack(
-        lambda r: features[r].astype(F32), f_left, f_right, packed, WIDTH
-    )
-    for s in range(2):
-        prepare(s, qkv_weight, agg_depth, agg_group, qkv_w, agg_w, grp_w, stack)
-    head_w[...] = jnp.zeros_like(head_w)
-    for a in range(3):
-        for b in range(3):
-            at = 8 * (3 * a + b)
-            head_w[at : at + 4] = head_weight[a, b].astype(F32)
-    edge3[...] = inside(14, 3, 128) * (1.0 / 6.0)
-    edge2[...] = inside(12, 2, 128)
     xp[...] = jnp.zeros_like(xp)
     joined[...] = jnp.zeros_like(joined)
     part[...] = jnp.zeros_like(part)
+    head_w[...] = jnp.zeros_like(head_w)
+    edge3[...] = inside(14, 3, 128) * (1.0 / 6.0)
+    edge2[...] = inside(12, 2, 128)
+    loads[0].wait()
+    pack(lambda r: features[r].astype(F32), f_left, f_right, packed, WIDTH)
     entered()
-
     first = trade(
         features, f_left, f_right, 3, f_across, f_sides, f_corners, hs_send.at[2], hs_recv.at[2]
     )
     for copy in first:
         copy.start()
+    for dz in (1, -1):
+        tell(ring.at[0], along(dz))
+    for copy in loads[1:]:
+        copy.wait()
+    prepare(qkv_weight, agg_depth, agg_group, qkv_w, agg_w, grp_w, stack)
+    for a in range(3):
+        for b in range(3):
+            at = 8 * (3 * a + b)
+            head_w[at : at + 4] = head_weight[a, b].astype(F32)
+    pl.semaphore_wait(ring.at[0], 2)
+    for dz in (2, -2):
+        tell(ring.at[1], along(dz))
     for copy in first:
         copy.wait()
     assemble(xp, features, 3, f_across, f_sides, f_corners)
@@ -299,7 +321,7 @@
                 here = slice(128 * l, 128 * l + 128)
                 lanes = pl.ds(pl.multiple_of(c * CHUNK + 128 * l, 128), 128)
                 taps = [
-                    [depth_weight[s, a, b : b + 1, lanes] for b in range(3)] for a in range(3)
+                    [depth_weight[a, b, s : s + 1, lanes] for b in range(3)] for a in range(3)
                 ]
                 bias = depth_bias[s : s + 1, lanes]
                 for pair in range(6):
@@ -327,6 +349,10 @@
             return carry
 
         lax.fori_loop(0, EXPANDED // CHUNK, expand, 0)
+        if s == 0:
+            pl.semaphore_wait(ring.at[1], 2)
+            for dz in (4, -4):
+                tell(ring.at[2], along(dz))
         bias = project_bias[s : s + 1]
         for r in range(12):
             here = slice(PITCH * r, PITCH * r + PITCH)
@@ -436,6 +462,8 @@
 
         arrived(got, 31, 0)
         mine[s] = jnp.sum(got[s], axis=0)
+        if s == 0:
+            pl.semaphore_wait(ring.at[2], 2)
         each(15, send2)
         deep[s, depth] = mine[s]
         for copy in swap:
@@ -515,12 +543,16 @@
 
 
 def local(*args):
+    args = list(args)
+    for i in (3, 8):
+        args[i] = jnp.transpose(args[i], (1, 2, 0, 3))
     dma = pltpu.SemaphoreType.DMA
     vmem = pltpu.VMEM
     area = 14 * PITCH
     inner = 12 * PITCH
     wide = 3 * WIDTH
-    scratch = [
+    held = [vmem(a.shape, a.dtype) for a in args[:13]] + [pltpu.SMEM((4,), F32)]
+    scratch = held + [
         vmem((area, WIDTH), F32),
         vmem((area, WIDTH), BF16),
         vmem((area, 128), F32),
@@ -534,9 +566,9 @@
         vmem((inner, WIDTH), F32),
         vmem((area, wide), F32),
         vmem((2, WIDTH, wide), BF16),
-        vmem((2, 48, wide), F32),
+        vmem((2, 40, wide), F32),
         vmem((2, 3, WIDTH, WIDTH), BF16),
-        vmem((144, wide), F32),
+        vmem((80, wide), F32),
         vmem((72, WIDTH), F32),
         vmem((2, 32, wide), F32),
         vmem((2, 32, wide), BF16),
@@ -563,6 +595,8 @@
         dma((3, 8)),
         dma((2, 3)),
         dma((2, 3)),
+        pltpu.SemaphoreType.REGULAR((3,)),
+        dma((14,)),
     ]
     in_vmem = pl.BlockSpec(memory_space=pltpu.VMEM)
     return pl.pallas_call(
@@ -571,11 +605,11 @@
             jax.ShapeDtypeStruct((ROWS, COLS, WIDTH), BF16),
             jax.ShapeDtypeStruct((4, ROWS, COLS), F32),
         ),
-        in_specs=[in_vmem] * 13 + [pl.BlockSpec(memory_space=pltpu.SMEM)],
+        in_specs=[pl.BlockSpec(memory_space=pl.ANY)] * 14,
         out_specs=(in_vmem, in_vmem),
         scratch_shapes=scratch,
         compiler_params=pltpu.CompilerParams(
-            collective_id=0, has_side_effects=True, vmem_limit_bytes=48 * 1024 * 1024
+            collective_id=0, has_side_effects=True, vmem_limit_bytes=60 * 1024 * 1024
         ),
     )(*args)
 

time: 84.1 us -> 76.2 us (0.906)
  local copies, waits for them, and re-layouts: 8.73 us -> 2.18 us
  Pallas kernels: 74.3 us -> 73.2 us
    unnamed x28 -> x4, local copies, waits for them, and re-layouts: 8.73 us -> 2.18 us
    pallas_call x1, Pallas kernels: 74.3 us -> 73.2 us  [local(): pl.pallas_call(kernel, out_shape=(jax.ShapeDtypeStruct((ROWS, COLS, WIDTH...]
where the time goes in v2:
time: 76.2 us; the launch traced here: 76 us
  Pallas kernels  73.2 us (96%)
  local copies, waits for them, and re-layouts  2.18 us (3%)
    pallas_call x1, Pallas kernels, local(): pl.pallas_call(kernel, out_shape=(jax.ShapeDtypeStruct((ROWS, COLS, WIDTH...  73.2 us
    unnamed x4, local copies, waits for them, and re-layouts  2.18 us

profile of v2, /device:TPU:1, one launch (start us, length us, event | category | flops | bytes accessed | tf_op | source)
XLA Modules:
  0.0 76.0 jit_solution(12227024809813539600)
XLA Ops:
  0.6 73.2 %shard_map.149 = (bf16[8,32,256]{2,1,0:T(8,128)(2,1)}, f32[4,8,32]{2,1,0:T(8,128)}) custom-call(bf16[8,32,256]{2,1,0:T(8,128)(2,1)} %refs_0_.1, bf16[2,256,1024]{2,1,0:T(8,128)(2,1)} %refs_1_.1, f32[2,1024]{1,0:T(2,128)} %refs_2_.1, f32[3,3,2,1024]{3,2,1,0:T(2,128)} %bitcast.3, f32[2,1024]{1,0:T(2,128)} %refs_4_.1, bf16[2,1024,256]{2,1,0:T(8,128)(2,1)} %refs_5_.1, ...), custom_call_target="tpu_custom_call" | custom-call | tf_op jit(solution)/shard_map/pallas_call | solution.py:602
  73.8 0.0 copy-start
  73.8 1.6 %copy.18 = bf16[8,32,256]{2,1,0:T(8,128)(2,1)} copy(bf16[8,32,256]{2,1,0:T(8,128)(2,1)} %get-tuple-element.4) | data formatting | bytes 262144
  75.4 0.0 copy-done
  75.4 0.6 copy.19
Async XLA Ops:
  73.8 1.6 %copy-start = (f32[4,8,32]{2,1,0:T(8,128)S(1)}, f32[4,8,32]{2,1,0:T(8,128)}, u32[]{:S(2)}) copy-start(f32[4,8,32]{2,1,0:T(8,128)} %get-tuple-element.5) | copy-start | bytes 12292

commit v3 on v2

--- a/solution.py
+++ b/solution.py
@@ -30,29 +30,35 @@
     return lax.rem(r + 16 + dr, 16), lax.rem(c + 32 + dc, 32)
 
 
-def far_first(k, half):
-    return half + (1 - 2 * lax.rem(k, 2)) * ((k + 1) // 2)
-
-
 def plane_of(r, c):
     return r * 2 + lax.rem(c, 2)
 
 
-def plane_peer(k):
+def hops(step, around):
+    return min(step, around - step)
+
+
+PLANE = sorted(
+    [(x, y, k) for x in range(4) for y in range(4) for k in range(2) if x or y or k],
+    key=lambda step: -hops(step[0], 4) - hops(step[1], 4),
+)
+DEPTH = sorted(range(1, 16), key=lambda step: -hops(step, 16))
+
+
+def plane_peers():
     r, c = spot()
-    dx = far_first(k // 8, 2)
-    dy = far_first(lax.rem(k // 2, 4), 2)
-    dk = 1 - lax.rem(k, 2)
-    x = lax.rem(r // 4 + dx, 4)
-    y = lax.rem(lax.rem(c, 2) * 2 + lax.rem(r // 2, 2) + dy, 4)
-    core = lax.rem(r + dk, 2)
-    return x * 4 + lax.rem(y, 2) * 2 + core, (c // 2) * 2 + y // 2
-
-
-def depth_peer(k):
-    r, c = spot()
-    z = lax.rem(c // 2 + far_first(k, 8), 16)
-    return r, z * 2 + lax.rem(c, 2)
+    y = lax.rem(c, 2) * 2 + lax.rem(r // 2, 2)
+    k = lax.rem(r, 2)
+    first = [lax.rem(r // 4 + step, 4) * 4 for step in range(4)]
+    ys = [lax.rem(y + step, 4) for step in range(4)]
+    second = [lax.rem(at, 2) * 2 for at in ys]
+    cols = [(c // 2) * 2 + at // 2 for at in ys]
+    cores = [k, 1 - k]
+    return [(first[x] + second[y] + cores[k], cols[y]) for x, y, k in PLANE]
+
+
+def depth_peers():
+    return [along(step) for step in DEPTH]
 
 
 AROUND = [(-1, 0), (1, 0), (0, -1), (0, 1), (-1, -1), (-1, 1), (1, -1), (1, 1)]
@@ -79,7 +85,8 @@
     barrier = pltpu.get_barrier_semaphore()
     for dr, dc in AROUND:
         tell(barrier, beside(dr, dc))
-    each(31, lambda k: tell(barrier, plane_peer(k)))
+    for device in plane_peers():
+        tell(barrier, device)
     for dz in (1, -1):
         tell(barrier, along(dz))
 
@@ -308,47 +315,43 @@
 
     for s in range(2):
         halo = HALOS[s]
-        acc[...] = jnp.zeros_like(acc)
-
-        def expand(c, carry, s=s):
-            wide = pl.ds(pl.multiple_of(c * CHUNK, CHUNK), CHUNK)
-            value = gate(dot(xb[...], expand_weight[s, :, wide]) + expand_bias[s : s + 1, wide])
+        def grow(c, lanes, s=s):
+            value = gate(dot(xb[...], expand_weight[s, :, lanes]) + expand_bias[s : s + 1, lanes])
             for l in range(CHUNK // 128):
-                hidden[:, 128 * l : 128 * l + 128] = (
+                hidden[c, :, 128 * l : 128 * l + 128] = (
                     value[:, 128 * l : 128 * l + 128] * edge3[...]
                 )
+
+        def filter3(source, lanes, s=s):
+            taps = [[depth_weight[a, b, s : s + 1, lanes] for b in range(3)] for a in range(3)]
+            bias = depth_bias[s : s + 1, lanes]
+            for pair in range(6):
+                done = []
+                for r in (2 * pair, 2 * pair + 1):
+                    rows = [source(PITCH * (r + a)) for a in range(3)]
+                    cols = [
+                        rows[0] * taps[0][b] + rows[1] * taps[1][b] + rows[2] * taps[2][b]
+                        for b in range(3)
+                    ]
+                    value = (
+                        cols[0]
+                        + pltpu.roll(cols[1], PITCH - 1, 0)
+                        + pltpu.roll(cols[2], PITCH - 2, 0)
+                        + bias
+                    )
+                    done.append(gate(value))
+                spread[2 * PITCH * pair : 2 * PITCH * (pair + 1), lanes] = jnp.concatenate(
+                    done, axis=0
+                ).astype(BF16)
+
+        for c in range(EXPANDED // CHUNK):
+            grow(c, slice(c * CHUNK, c * CHUNK + CHUNK))
             for l in range(CHUNK // 128):
-                here = slice(128 * l, 128 * l + 128)
-                lanes = pl.ds(pl.multiple_of(c * CHUNK + 128 * l, 128), 128)
-                taps = [
-                    [depth_weight[a, b, s : s + 1, lanes] for b in range(3)] for a in range(3)
-                ]
-                bias = depth_bias[s : s + 1, lanes]
-                for pair in range(6):
-                    done = []
-                    for r in (2 * pair, 2 * pair + 1):
-                        rows = [
-                            hidden[PITCH * (r + a) : PITCH * (r + a) + PITCH, here]
-                            for a in range(3)
-                        ]
-                        cols = [
-                            rows[0] * taps[0][b] + rows[1] * taps[1][b] + rows[2] * taps[2][b]
-                            for b in range(3)
-                        ]
-                        value = (
-                            cols[0]
-                            + pltpu.roll(cols[1], PITCH - 1, 0)
-                            + pltpu.roll(cols[2], PITCH - 2, 0)
-                            + bias
-                        )
-                        done.append(gate(value) * (1.0 / 6.0))
-                    spread[2 * PITCH * pair : 2 * PITCH * (pair + 1), here] = jnp.concatenate(
-                        done, axis=0
-                    ).astype(BF16)
-            acc[...] += dot(spread[...], project_weight[s, wide, :])
-            return carry
-
-        lax.fori_loop(0, EXPANDED // CHUNK, expand, 0)
+                filter3(
+                    lambda at, c=c, l=l: hidden[c, at : at + PITCH, 128 * l : 128 * l + 128],
+                    slice(c * CHUNK + 128 * l, c * CHUNK + 128 * l + 128),
+                )
+        acc[...] = dot(spread[...], project_weight[s]) * (1.0 / 6.0)
         if s == 0:
             pl.semaphore_wait(ring.at[1], 2)
             for dz in (4, -4):
@@ -415,16 +418,6 @@
                 device_id_type=MESH,
             )
 
-        def send1(k, s=s):
-            device = plane_peer(k)
-            remote(part.at[s, plane_of(*device)], got.at[s, me], 0, device).start()
-
-        def send2(k, s=s):
-            remote(mine.at[s], deep.at[s, depth], 1, depth_peer(k)).start()
-
-        def send3(k, s=s):
-            remote(total.at[s], whole.at[s, me], 2, plane_peer(k)).start()
-
         def arrived(buffer, count, stage, s=s):
             view = buffer.at[s, pl.ds(0, count)]
             pltpu.make_async_copy(view, view, ar_recv.at[s, stage]).wait()
@@ -433,7 +426,8 @@
             view = buffer.at[s, pl.ds(0, count)]
             pltpu.make_async_copy(view, view, ar_send.at[s, stage]).wait()
 
-        each(31, send1)
+        for device in plane_peers():
+            remote(part.at[s, plane_of(*device)], got.at[s, me], 0, device).start()
         got[s, me] = part[s, me]
 
         lax.fori_loop(0, 2, taps5, 0)
@@ -464,18 +458,20 @@
         mine[s] = jnp.sum(got[s], axis=0)
         if s == 0:
             pl.semaphore_wait(ring.at[2], 2)
-        each(15, send2)
+        for device in depth_peers():
+            remote(mine.at[s], deep.at[s, depth], 1, device).start()
         deep[s, depth] = mine[s]
         for copy in swap:
             copy.start()
+        arrived(deep, 15, 1)
+        total[s] = jnp.sum(deep[s], axis=0)
+        for device in plane_peers():
+            remote(total.at[s], whole.at[s, me], 2, device).start()
+        whole[s, me] = total[s]
         for copy in swap:
             copy.wait()
         area = (ROWS + 2 * halo) * PITCH
         assemble(joined.at[pl.ds(0, area)], tile.at[s], halo, across, sides.at[s], corners.at[s])
-        arrived(deep, 15, 1)
-        total[s] = jnp.sum(deep[s], axis=0)
-        each(31, send3)
-        whole[s, me] = total[s]
         arrived(whole, 31, 2)
         sent(got, 31, 0)
         sent(deep, 15, 1)
@@ -557,8 +553,8 @@
         vmem((area, WIDTH), BF16),
         vmem((area, 128), F32),
         vmem((inner, 128), F32),
-        vmem((area, CHUNK), F32),
-        vmem((inner, CHUNK), BF16),
+        vmem((EXPANDED // CHUNK, area, CHUNK), F32),
+        vmem((inner, EXPANDED), BF16),
         vmem((inner, WIDTH), F32),
         vmem((inner, wide), F32),
         vmem((ROWS * COLS, wide), BF16),

time: 76.2 us -> 68.4 us (0.90)
  Pallas kernels: 73.2 us -> 65.5 us
    pallas_call x1, Pallas kernels: 73.2 us -> 65.5 us  [local(): pl.pallas_call(kernel, out_shape=(jax.ShapeDtypeStruct((ROWS, COLS, WIDTH...]
where the time goes in v3:
time: 68.4 us; the launch traced here: 68.3 us
  Pallas kernels  65.5 us (96%)
  local copies, waits for them, and re-layouts  2.18 us (3%)
    pallas_call x1, Pallas kernels, local(): pl.pallas_call(kernel, out_shape=(jax.ShapeDtypeStruct((ROWS, COLS, WIDTH...  65.5 us
    unnamed x4, local copies, waits for them, and re-layouts  2.18 us

profile of v3, /device:TPU:1, one launch (start us, length us, event | category | flops | bytes accessed | tf_op | source)
XLA Modules:
  0.0 68.3 jit_solution(17366294541986215343)
XLA Ops:
  0.6 65.5 %shard_map.149 = (bf16[8,32,256]{2,1,0:T(8,128)(2,1)}, f32[4,8,32]{2,1,0:T(8,128)}) custom-call(bf16[8,32,256]{2,1,0:T(8,128)(2,1)} %refs_0_.1, bf16[2,256,1024]{2,1,0:T(8,128)(2,1)} %refs_1_.1, f32[2,1024]{1,0:T(2,128)} %refs_2_.1, f32[3,3,2,1024]{3,2,1,0:T(2,128)} %bitcast.3, f32[2,1024]{1,0:T(2,128)} %refs_4_.1, bf16[2,1024,256]{2,1,0:T(8,128)(2,1)} %refs_5_.1, ...), custom_call_target="tpu_custom_call" | custom-call | tf_op jit(solution)/shard_map/pallas_call | solution.py:598
  66.1 0.0 copy-start
  66.1 1.6 %copy.18 = bf16[8,32,256]{2,1,0:T(8,128)(2,1)} copy(bf16[8,32,256]{2,1,0:T(8,128)(2,1)} %get-tuple-element.4) | data formatting | bytes 262144
  67.7 0.0 copy-done
  67.7 0.6 copy.19
Async XLA Ops:
  66.1 1.6 %copy-start = (f32[4,8,32]{2,1,0:T(8,128)S(1)}, f32[4,8,32]{2,1,0:T(8,128)}, u32[]{:S(2)}) copy-start(f32[4,8,32]{2,1,0:T(8,128)} %get-tuple-element.5) | copy-start | bytes 12292

commit v4 on v3

--- a/solution.py
+++ b/solution.py
@@ -61,7 +61,7 @@
     return [along(step) for step in DEPTH]
 
 
-AROUND = [(-1, 0), (1, 0), (0, -1), (0, 1), (-1, -1), (-1, 1), (1, -1), (1, 1)]
+AROUND = [(-1, -1), (-1, 1), (1, -1), (1, 1), (0, -1), (0, 1), (-1, 0), (1, 0)]
 
 
 def each(count, body):
@@ -129,14 +129,14 @@
     top = pl.ds(0, 16)
     bottom = pl.ds(16, 16)
     plan = [
-        ((1, 0), low, across.at[0]),
-        ((-1, 0), high, across.at[1]),
-        ((0, 1), right, sides.at[0]),
-        ((0, -1), left, sides.at[1]),
         ((1, 1), right.at[bottom], corners.at[0]),
         ((1, -1), left.at[bottom], corners.at[1]),
         ((-1, 1), right.at[top], corners.at[2]),
         ((-1, -1), left.at[top], corners.at[3]),
+        ((0, 1), right, sides.at[0]),
+        ((0, -1), left, sides.at[1]),
+        ((1, 0), low, across.at[0]),
+        ((-1, 0), high, across.at[1]),
     ]
     return [
         pltpu.make_async_remote_copy(
@@ -243,6 +243,9 @@
         center,
         mixed,
         joined,
+        asked,
+        blocks01,
+        unit,
         qkv_w,
         agg_w,
         grp_w,
@@ -279,15 +282,8 @@
     loads = [
         pltpu.make_async_copy(src, dst, load.at[i]) for i, (src, dst) in enumerate(zip(given, held))
     ]
-    for copy in loads:
-        copy.start()
+    loads[0].start()
     enter()
-    xp[...] = jnp.zeros_like(xp)
-    joined[...] = jnp.zeros_like(joined)
-    part[...] = jnp.zeros_like(part)
-    head_w[...] = jnp.zeros_like(head_w)
-    edge3[...] = inside(14, 3, 128) * (1.0 / 6.0)
-    edge2[...] = inside(12, 2, 128)
     loads[0].wait()
     pack(lambda r: features[r].astype(F32), f_left, f_right, packed, WIDTH)
     entered()
@@ -296,8 +292,20 @@
     )
     for copy in first:
         copy.start()
+    for copy in loads[1:]:
+        copy.start()
     for dz in (1, -1):
         tell(ring.at[0], along(dz))
+    xp[...] = jnp.zeros_like(xp)
+    joined[...] = jnp.zeros_like(joined)
+    part[...] = jnp.zeros_like(part)
+    head_w[...] = jnp.zeros_like(head_w)
+    edge3[...] = inside(14, 3, 128) * (1.0 / 6.0)
+    edge2[...] = inside(12, 2, 128)
+    i = lax.broadcasted_iota(jnp.int32, (WIDTH, WIDTH), 0)
+    j = lax.broadcasted_iota(jnp.int32, (WIDTH, WIDTH), 1)
+    blocks01[...] = jnp.where(i // HD == j // HD, 1.0, 0.0)
+    unit[...] = jnp.where(i == j, 1.0, 0.0)
     for copy in loads[1:]:
         copy.wait()
     prepare(qkv_weight, agg_depth, agg_group, qkv_w, agg_w, grp_w, stack)
@@ -364,10 +372,11 @@
             for l in range(WIDTH // 128):
                 lanes = slice(128 * l, 128 * l + 128)
                 mixed[here, lanes] = value[:, lanes] * edge2[here]
-        qkv[...] = dot(mixed[...].astype(BF16), qkv_w[s])
-
-        def taps5(l, carry, s=s):
-            lanes = pl.ds(pl.multiple_of(l * 128, 128), 128)
+        source = mixed[...].astype(BF16)
+        qkv[:, WIDTH:] = dot(source, qkv_w[s, :, WIDTH:])
+
+        def taps5(l, s=s):
+            lanes = slice(l * 128, l * 128 + 128)
             for r in range(ROWS):
                 cols = [None] * 5
                 for a in range(5):
@@ -381,13 +390,13 @@
                 scaled[COLS * r : COLS * r + COLS, lanes] = value[0:COLS].astype(BF16)
                 near = pltpu.roll(qkv[PITCH * (r + 2) : PITCH * (r + 3), lanes], PITCH - 2, 0)
                 center[COLS * r : COLS * r + COLS, lanes] = near[0:COLS].astype(BF16)
-            return carry
 
         def kind(t):
             lanes = slice(WIDTH * t, WIDTH * t + WIDTH)
             return [center[:, lanes], dot(scaled[:, lanes], grp_w[s, t]).astype(BF16)]
 
-        lax.fori_loop(2, 6, taps5, 0)
+        for l in range(2, 6):
+            taps5(l)
         lane = lax.broadcasted_iota(jnp.int32, (HD, 128), 1) // HD
         ones = jnp.ones((16, ROWS * COLS), BF16)
         for branch, (k, v) in enumerate(zip(kind(1), kind(2))):
@@ -430,7 +439,9 @@
             remote(part.at[s, plane_of(*device)], got.at[s, me], 0, device).start()
         got[s, me] = part[s, me]
 
-        lax.fori_loop(0, 2, taps5, 0)
+        qkv[:, 0:WIDTH] = dot(mixed[...].astype(BF16), qkv_w[s, :, 0:WIDTH])
+        for l in range(2):
+            taps5(l)
         near, far = kind(0)
         for r in range(ROWS):
             here = slice(COLS * r, COLS * r + COLS)
@@ -472,6 +483,7 @@
             copy.wait()
         area = (ROWS + 2 * halo) * PITCH
         assemble(joined.at[pl.ds(0, area)], tile.at[s], halo, across, sides.at[s], corners.at[s])
+        asked[0:area] = joined[0:area, WIDTH:].astype(BF16)
         arrived(whole, 31, 2)
         sent(got, 31, 0)
         sent(deep, 15, 1)
@@ -479,10 +491,8 @@
 
         for p in range(32):
             table[4 * p : 4 * p + 4, :] = whole[s, p, 0:4, :]
-        i = lax.broadcasted_iota(jnp.int32, (WIDTH, WIDTH), 0)
-        j = lax.broadcasted_iota(jnp.int32, (WIDTH, WIDTH), 1)
-        same = i // HD == j // HD
-        ones = jnp.where(same, 1.0, 0.0).astype(BF16)
+        same = blocks01[...]
+        ones = same.astype(BF16)
         attended = []
         for branch in range(2):
             blocks = []
@@ -491,12 +501,11 @@
                 block = table[HD * group : HD * group + HD]
                 blocks.append(jnp.concatenate([block] * 4, axis=0))
                 keys[0:1, 128 * g : 128 * g + 128] = whole[s, group, 4:5, :]
-            numer_w = jnp.where(
-                same, jnp.concatenate([jnp.concatenate([b, b], axis=1) for b in blocks], axis=0), 0.0
+            numer_w = same * jnp.concatenate(
+                [jnp.concatenate([b, b], axis=1) for b in blocks], axis=0
             )
-            key_row = jnp.broadcast_to(keys[0:1, :], (WIDTH, WIDTH))
-            denom_w = dot(jnp.where(i == j, key_row, 0.0).astype(BF16), ones)
-            q = joined[0:area, WIDTH * (1 + branch) : WIDTH * (2 + branch)].astype(BF16)
+            denom_w = dot((unit[...] * keys[0:1, :]).astype(BF16), ones)
+            q = asked[0:area, WIDTH * branch : WIDTH * (branch + 1)]
             numer = dot(q, numer_w.astype(BF16))
             denom = dot(q, denom_w.astype(BF16))
             attended.append((numer / (denom + 1e-06)).astype(BF16))
@@ -561,6 +570,9 @@
         vmem((ROWS * COLS, wide), BF16),
         vmem((inner, WIDTH), F32),
         vmem((area, wide), F32),
+        vmem((area, 2 * WIDTH), BF16),
+        vmem((WIDTH, WIDTH), F32),
+        vmem((WIDTH, WIDTH), F32),
         vmem((2, WIDTH, wide), BF16),
         vmem((2, 40, wide), F32),
         vmem((2, 3, WIDTH, WIDTH), BF16),

time: 68.4 us -> 68.3 us (level)
  no operation moved by 1% of the time
where the time goes in v4:
time: 68.3 us; the launch traced here: 68.1 us
  Pallas kernels  65.3 us (96%)
  local copies, waits for them, and re-layouts  2.18 us (3%)
    pallas_call x1, Pallas kernels, local(): pl.pallas_call(kernel, out_shape=(jax.ShapeDtypeStruct((ROWS, COLS, WIDTH...  65.3 us
    unnamed x4, local copies, waits for them, and re-layouts  2.18 us

profile of v4, /device:TPU:1, one launch (start us, length us, event | category | flops | bytes accessed | tf_op | source)
XLA Modules:
  0.0 68.1 jit_solution(840171230914666141)
XLA Ops:
  0.6 65.3 %shard_map.149 = (bf16[8,32,256]{2,1,0:T(8,128)(2,1)}, f32[4,8,32]{2,1,0:T(8,128)}) custom-call(bf16[8,32,256]{2,1,0:T(8,128)(2,1)} %refs_0_.1, bf16[2,256,1024]{2,1,0:T(8,128)(2,1)} %refs_1_.1, f32[2,1024]{1,0:T(2,128)} %refs_2_.1, f32[3,3,2,1024]{3,2,1,0:T(2,128)} %bitcast.3, f32[2,1024]{1,0:T(2,128)} %refs_4_.1, bf16[2,1024,256]{2,1,0:T(8,128)(2,1)} %refs_5_.1, ...), custom_call_target="tpu_custom_call" | custom-call | tf_op jit(solution)/shard_map/pallas_call | solution.py:610
  65.9 0.0 copy-start
  65.9 1.6 %copy.18 = bf16[8,32,256]{2,1,0:T(8,128)(2,1)} copy(bf16[8,32,256]{2,1,0:T(8,128)(2,1)} %get-tuple-element.4) | data formatting | bytes 262144
  67.5 0.0 copy-done
  67.5 0.6 copy.19
Async XLA Ops:
  65.9 1.6 %copy-start = (f32[4,8,32]{2,1,0:T(8,128)S(1)}, f32[4,8,32]{2,1,0:T(8,128)}, u32[]{:S(2)}) copy-start(f32[4,8,32]{2,1,0:T(8,128)} %get-tuple-element.5) | copy-start | bytes 12292

commit v5 on v4

--- a/solution.py
+++ b/solution.py
@@ -375,8 +375,8 @@
         source = mixed[...].astype(BF16)
         qkv[:, WIDTH:] = dot(source, qkv_w[s, :, WIDTH:])
 
-        def taps5(l, s=s):
-            lanes = slice(l * 128, l * 128 + 128)
+        def taps5(l, carry, s=s):
+            lanes = pl.ds(pl.multiple_of(l * 128, 128), 128)
             for r in range(ROWS):
                 cols = [None] * 5
                 for a in range(5):
@@ -390,13 +390,13 @@
                 scaled[COLS * r : COLS * r + COLS, lanes] = value[0:COLS].astype(BF16)
                 near = pltpu.roll(qkv[PITCH * (r + 2) : PITCH * (r + 3), lanes], PITCH - 2, 0)
                 center[COLS * r : COLS * r + COLS, lanes] = near[0:COLS].astype(BF16)
+            return carry
 
         def kind(t):
             lanes = slice(WIDTH * t, WIDTH * t + WIDTH)
             return [center[:, lanes], dot(scaled[:, lanes], grp_w[s, t]).astype(BF16)]
 
-        for l in range(2, 6):
-            taps5(l)
+        lax.fori_loop(2, 6, taps5, 0)
         lane = lax.broadcasted_iota(jnp.int32, (HD, 128), 1) // HD
         ones = jnp.ones((16, ROWS * COLS), BF16)
         for branch, (k, v) in enumerate(zip(kind(1), kind(2))):
@@ -440,8 +440,7 @@
         got[s, me] = part[s, me]
 
         qkv[:, 0:WIDTH] = dot(mixed[...].astype(BF16), qkv_w[s, :, 0:WIDTH])
-        for l in range(2):
-            taps5(l)
+        lax.fori_loop(0, 2, taps5, 0)
         near, far = kind(0)
         for r in range(ROWS):
             here = slice(COLS * r, COLS * r + COLS)

time: 68.3 us -> 68.3 us (level)
  no operation moved by 1% of the time
where the time goes in v5:
time: 68.3 us; the launch traced here: 68.1 us
  Pallas kernels  65.3 us (96%)
  local copies, waits for them, and re-layouts  2.18 us (3%)
    pallas_call x1, Pallas kernels, local(): pl.pallas_call(kernel, out_shape=(jax.ShapeDtypeStruct((ROWS, COLS, WIDTH...  65.3 us
    unnamed x4, local copies, waits for them, and re-layouts  2.18 us

profile of v5, /device:TPU:1, one launch (start us, length us, event | category | flops | bytes accessed | tf_op | source)
XLA Modules:
  0.0 68.1 jit_solution(2348521195715380840)
XLA Ops:
  0.6 65.3 %shard_map.149 = (bf16[8,32,256]{2,1,0:T(8,128)(2,1)}, f32[4,8,32]{2,1,0:T(8,128)}) custom-call(bf16[8,32,256]{2,1,0:T(8,128)(2,1)} %refs_0_.1, bf16[2,256,1024]{2,1,0:T(8,128)(2,1)} %refs_1_.1, f32[2,1024]{1,0:T(2,128)} %refs_2_.1, f32[3,3,2,1024]{3,2,1,0:T(2,128)} %bitcast.3, f32[2,1024]{1,0:T(2,128)} %refs_4_.1, bf16[2,1024,256]{2,1,0:T(8,128)(2,1)} %refs_5_.1, ...), custom_call_target="tpu_custom_call" | custom-call | tf_op jit(solution)/shard_map/pallas_call | solution.py:609
  66.0 0.0 copy-start
  66.0 1.6 %copy.18 = bf16[8,32,256]{2,1,0:T(8,128)(2,1)} copy(bf16[8,32,256]{2,1,0:T(8,128)(2,1)} %get-tuple-element.4) | data formatting | bytes 262144
  67.5 0.0 copy-done
  67.5 0.6 copy.19
Async XLA Ops:
  66.0 1.6 %copy-start = (f32[4,8,32]{2,1,0:T(8,128)S(1)}, f32[4,8,32]{2,1,0:T(8,128)}, u32[]{:S(2)}) copy-start(f32[4,8,32]{2,1,0:T(8,128)} %get-tuple-element.5) | copy-start | bytes 12292
